TPU v7x, 1024 devices: a whole 4x8x16 slice. The times are simulated.
1024 devices in a mesh: dp: 32 (over z, core), node: 4 (over x), local: 8 (over y).
Axes of the slice: x: 4, y: 8, z: 16, core: 2. Of those that a mesh axis runs over, the one named last changes fastest.
Arguments:
- grad_out: bfloat16 [131072, 7168], P(('dp', 'node', 'local')), parts along dimension 0, may hold values from -6 to 6
- probs: float32 [131072], P(('dp', 'node', 'local')), parts along dimension 0, may hold values from 0.05 to 1
- expert_ids: int32 [131072], P(('dp', 'node', 'local')), parts along dimension 0, may hold values from 0 to 3, as said below
- slot_ids: int32 [131072], P(('dp', 'node', 'local')), parts along dimension 0, may hold values from 0 to 33
- w_down: bfloat16 [4, 2048, 7168], P('node', None, 'local'), may hold values from -0.125 to 0.125
- hidden: bfloat16 [128, 2048, 1088], P(('dp', 'node'), 'local'), parts along dimension 0, may hold values from -0.29882812 to 0.29882812
Outputs:
- d_hidden: bfloat16 [128, 2048, 1088], P(('dp', 'node'), 'local'), parts along dimension 0
- d_probs: float32 [131072], P(('dp', 'node', 'local')), parts along dimension 0
There are 32 independent parts, one for each index of `dp`. A program takes and returns all parts, laid end to end along the dimension named above; an argument that names none is the same for every part. Nothing has to cross between parts.
Inputs may be any that keep to these rules, and one draw needn't show every extreme that they name: `expert_ids`: among the tokens of one device no two share both expert and slot; every expert receives tokens of every device, and in every draw one expert receives 34 tokens of every device.
All inputs are finite; a program needn't handle non-finite values.
Results may differ from a plain program's by a relative error of at most 0.02.
Values may be sent and summed in bfloat16 or wider, within the bound.
A program may use at most 32 MiB of HBM per device.

v0:
```python
import jax
import jax.numpy as jnp
from jax import lax
from jax.sharding import PartitionSpec as P


def body(grad_out, probs, expert_ids, slot_ids, w_down, hidden):
    tok_rows = grad_out.shape[0]
    n_node = lax.axis_size("node")
    n_local = lax.axis_size("local")
    cells = hidden.shape[2]
    sources = n_node * n_local
    per_source = cells // sources
    piece = w_down.shape[2]
    grad_three = grad_out.reshape(tok_rows, n_local, piece)
    wts_three = jnp.broadcast_to(probs.astype(jnp.bfloat16)[:, None], (tok_rows, n_local))
    send_rows = (
        jnp.zeros((n_node, n_local, per_source, piece), jnp.bfloat16)
        .at[expert_ids, :, slot_ids]
        .set(grad_three)
    )
    send_wts = (
        jnp.zeros((n_node, n_local, per_source), jnp.bfloat16)
        .at[expert_ids, :, slot_ids]
        .set(wts_three)
    )
    got_rows, got_wts = (
        lax.all_to_all(
            send_rows.reshape(sources, per_source, piece),
            ("node", "local"),
            split_axis=0,
            concat_axis=0,
            tiled=True,
        ),
        lax.all_to_all(
            send_wts.reshape(sources, per_source),
            ("node", "local"),
            split_axis=0,
            concat_axis=0,
            tiled=True,
        ),
    )
    received = got_rows.reshape(cells, piece)
    received_wts = got_wts.reshape(cells).astype(jnp.float32)
    weight_local = w_down[0]
    raw = lax.psum_scatter(
        lax.dot_general(
            weight_local, received, (((1,), (1,)), ((), ())), preferred_element_type=jnp.float32
        ).astype(jnp.bfloat16),
        "local",
        scatter_dimension=0,
        tiled=True,
    ).astype(jnp.float32)
    d_hidden = (raw * received_wts[None, :]).astype(jnp.bfloat16)[None]
    route_part = jnp.sum(hidden[0].astype(jnp.float32) * raw, axis=0)
    pieces = lax.all_to_all(
        route_part.reshape(sources, per_source),
        ("node", "local"),
        split_axis=0,
        concat_axis=0,
        tiled=True,
    )
    back = jnp.sum(pieces.reshape(n_node, n_local, per_source), axis=1)
    target = expert_ids * per_source + slot_ids
    picker = (target[:, None] == jnp.arange(n_node * per_source, dtype=jnp.int32)[None, :]).astype(
        jnp.float32
    )
    d_probs = jnp.dot(
        picker,
        back.reshape(-1),
        precision=lax.Precision.HIGHEST,
        preferred_element_type=jnp.float32,
    )
    return (d_hidden, d_probs)


def solution(mesh):
    return jax.shard_map(
        body,
        mesh=mesh,
        in_specs=(
            P(("dp", "node", "local"), None),
            P(("dp", "node", "local")),
            P(("dp", "node", "local")),
            P(("dp", "node", "local")),
            P("node", None, "local"),
            P(("dp", "node"), "local", None),
        ),
        out_specs=(P(("dp", "node"), "local", None), P(("dp", "node", "local"))),
        check_vma=False,
    )
```

profile of v0, /device:TPU:1, one launch (start us, length us, event | category | flops | bytes accessed | tf_op | source)
XLA Modules:
  0.0 196.7 jit_solution(17460152580502255023)
XLA Ops:
  7.2 0.0 copy-start.3
  7.2 0.0 copy-start.2
  7.2 0.0 reduce-scatter.2.cloned.1.call-start
  7.2 3.1 %copy.23 = bf16[16,8,8,896]{3,2,1,0:T(8,128)(2,1)} copy(bf16[16,8,8,896]{3,1,2,0:T(8,128)(2,1)} %bitcast.39) | data formatting | bytes 3670016
  10.3 0.0 copy-done.3
  10.3 0.0 copy-done.2
  10.3 0.1 broadcast_in_dim.12
  10.5 13.2 %scatter_fusion = bf16[4,8,34,896]{3,1,2,0:T(8,128)(2,1)S(1)} fusion(bf16[4,8,34,896]{3,1,2,0:T(8,128)(2,1)S(1)} %broadcast_in_dim.12, s32[128]{0:T(128)S(1)} %fusion.9, bf16[128,8,896]{2,1,0:T(8,128)(2,1)} %bitcast.38), kind=kCustom, calls=%fused_computation | custom fusion | bytes 5506048 | tf_op jit(solution)/shard_map/scatter | solution.py:20
  23.7 0.2 copy.25
  23.8 0.7 copy.20
  24.5 58.0 %all_to_all.23 = bf16[32,34,896]{2,1,0:T(8,128)(2,1)S(1)} all-to-all(bf16[32,34,896]{2,1,0:T(8,128)(2,1)S(1)} %copy.20), channel_id=1, replica_groups=mesh['dp'=32,'node'=4,'local'=8] {'node','local'}, dimensions={0} | all-to-all | bytes 3899392 | tf_op jit(solution)/shard_map/all_to_all | solution.py:28
  82.5 2.0 %reshape.43 = bf16[1088,896]{1,0:T(8,128)(2,1)} reshape(bf16[32,34,896]{2,1,0:T(8,128)(2,1)S(1)} %all_to_all.23) | data formatting | bytes 3899392 | tf_op jit(solution)/shard_map/reshape | solution.py:43
  84.6 9.5 %fusion = bf16[2048,1088]{0,1:T(8,128)(2,1)} fusion(bf16[1088,896]{1,0:T(8,128)(2,1)} %reshape.43, bf16[1,2048,896]{2,1,0:T(8,128)(2,1)} %param.10), kind=kOutput, calls=%fused_computation.3 | convolution fusion | flops 3995205632 | bytes 10076160 | tf_op jit(solution)/shard_map/dot_general | solution.py:47
  94.1 0.0 copy-start.1
  94.1 0.0 copy-start
  94.1 0.0 reduce-scatter.2.cloned.1.call-update
  94.1 0.6 copy-done.1
  94.7 0.1 broadcast_in_dim.30
  94.8 6.8 %scatter_fusion.1 = bf16[4,8,34]{1,0,2:T(4,128)(2,1)S(1)} fusion(bf16[4,8,34]{1,0,2:T(4,128)(2,1)S(1)} %broadcast_in_dim.29, s32[128]{0:T(128)S(1)} %fusion.9, bf16[128,8]{1,0:T(8,128)(2,1)S(1)} %broadcast_in_dim.30), kind=kCustom, calls=%fused_computation.1 | custom fusion | bytes 7168 | tf_op jit(solution)/shard_map/scatter | solution.py:25
  101.7 0.1 copy.21
  101.8 15.5 %all_to_all.24 = bf16[32,1,34]{2,1,0:T(2,128)(2,1)S(1)} all-to-all(bf16[32,1,34]{2,1,0:T(2,128)(2,1)S(1)} %copy.22), channel_id=1, replica_groups=mesh['dp'=32,'node'=4,'local'=8] {'node','local'}, dimensions={0} | all-to-all | bytes 4352 | tf_op jit(solution)/shard_map/all_to_all | solution.py:35
  117.3 0.1 convert_reduce_fusion
  117.3 0.1 reshape.46
  117.4 53.0 %reduce-scatter.2.cloned.1.call-done = bf16[256,1088]{0,1:T(8,128)(2,1)} async-done(((bf16[2048,1088]{0,1:T(8,128)(2,1)}), bf16[256,1088]{0,1:T(8,128)(2,1)}) %reduce-scatter.2.cloned.1.call-update) | async-done | bytes 557072 | tf_op jit(solution)/shard_map/reduce_scatter | solution.py:46
  170.5 0.0 copy-done
  170.5 2.2 %fusion.3 = (f32[1088]{0:T(1024)S(1)}, bf16[1,256,1088]{1,2,0:T(8,128)(2,1)}) fusion(bf16[256,1088]{0,1:T(8,128)(2,1)} %reduce-scatter.2.cloned.1.call-done, bf16[1,256,1088]{1,2,0:T(8,128)(2,1)S(1)} %copy-done, f32[1088]{0:T(1024)S(1)} %reshape.46), kind=kLoop, calls=%fused_computation.9 | loop fusion | flops 1670080 | bytes 1679872 | tf_op jit(solution)/shard_map/reduce_sum | solution.py:55
  172.7 0.7 all_to_all.18
  173.4 7.0 %all-to-all-start.2 = ((f32[32,1,34]{2,1,0:T(1,128)}), f32[32,1,34]{2,1,0:T(1,128)S(1)}, u32[]{:S(2)}, u32[]{:S(2)}) async-start(f32[32,1,34]{2,1,0:T(1,128)} %all_to_all.18), calls=%async_computation.3 | async-start | bytes 32768 | tf_op jit(solution)/shard_map/all_to_all | solution.py:56
  180.4 8.6 %all-to-all-done.2 = f32[32,1,34]{2,1,0:T(1,128)S(1)} async-done(((f32[32,1,34]{2,1,0:T(1,128)}), f32[32,1,34]{2,1,0:T(1,128)S(1)}, u32[]{:S(2)}, u32[]{:S(2)}) %all-to-all-start.2) | async-done | bytes 4384 | tf_op jit(solution)/shard_map/all_to_all | solution.py:56
  189.0 0.1 reshape.60
  189.1 0.8 convolution_bitcast_fusion
  (6 shorter events, 0.1 us)
Async XLA Ops:
  7.2 3.2 %copy-start.3 = (s32[128]{0:T(128)S(1)}, s32[128]{0:T(128)}, u32[]{:S(2)}) copy-start(s32[128]{0:T(128)} %param.8) | copy-start | bytes 1540
  7.2 3.1 %copy-start.2 = (s32[128]{0:T(128)S(1)}, s32[128]{0:T(128)}, u32[]{:S(2)}) copy-start(s32[128]{0:T(128)} %param.9) | copy-start | bytes 1540
  7.2 163.3 %reduce-scatter.2.cloned.1.call-start = ((), (), s32[]{:S(2)}) async-start(), calls=%async_computation.4 | async-start | bytes 5013504 | tf_op jit(solution)/shard_map/reduce_scatter | solution.py:46
  94.1 0.7 copy-start.1
  94.1 76.4 %copy-start = (bf16[1,256,1088]{1,2,0:T(8,128)(2,1)S(1)}, bf16[1,256,1088]{1,2,0:T(8,128)(2,1)}, u32[]{:S(2)}) copy-start(bf16[1,256,1088]{1,2,0:T(8,128)(2,1)} %param.11) | copy-start | bytes 1671172
  173.4 15.6 %all-to-all-start.2 = ((f32[32,1,34]{2,1,0:T(1,128)}), f32[32,1,34]{2,1,0:T(1,128)S(1)}, u32[]{:S(2)}, u32[]{:S(2)}) async-start(f32[32,1,34]{2,1,0:T(1,128)} %all_to_all.18), calls=%async_computation.3 | async-start | bytes 32768 | tf_op jit(solution)/shard_map/all_to_all | solution.py:56
Sparse Core Ops, SparseCore 0:
  94.2 76.2 reduce-scatter.1
where the time goes:
time: 197 us
  blocking collectives  73.5 us (37%)
  waiting for transfers between devices  61.7 us (31%)
  local copies, waits for them, and re-layouts  27.9 us (14%)
  between operations  14.1 us (7%)
  matrix products  10.3 us (5%)
  starting transfers between devices  7.04 us (4%)
  other arithmetic  2.25 us (1%)
    all_to_all x1, blocking collectives, body(): lax.all_to_all(send_rows.reshape(sources, per_source, piece), ('node', 'l...  58 us
    reduce_scatter x1, waiting for transfers between devices, body(): lax.psum_scatter(lax.dot_general(weight_local, received, (((1,), (1,)), (...  53 us
    all_to_all x1, blocking collectives, body(): lax.all_to_all(send_wts.reshape(sources, per_source), ('node', 'local'),...  15.5 us
    scatter x2, local copies, waits for them, and re-layouts, body(): send_rows = jnp.zeros((n_node, n_local, per_source, piece), jnp.bfloat16)...  13.3 us
    dot_general x1, matrix products, body(): lax.dot_general(weight_local, received, (((1,), (1,)), ((), ())), preferr...  9.48 us
    all_to_all x1, waiting for transfers between devices, body(): lax.all_to_all(route_part.reshape(sources, per_source), ('node', 'local')...  8.61 us
    all_to_all x1, starting transfers between devices, body(): lax.all_to_all(route_part.reshape(sources, per_source), ('node', 'local')...  7 us
    scatter x2, local copies, waits for them, and re-layouts, body(): send_wts = jnp.zeros((n_node, n_local, per_source), jnp.bfloat16).at[expe...  6.95 us
  transfers between devices with their start and end apart: 2, of which 2 were waited for; matrix products, arithmetic and copies ran while one was open for 4% of the time, Pallas kernels for 0%

commit v1 on v0

v1 whole, which is shorter than its diff:
```python
import functools

import jax
import jax.numpy as jnp
import numpy as np
from jax import lax
from jax.experimental import pallas as pl
from jax.experimental.pallas import tpu as pltpu
from jax.sharding import PartitionSpec as P

MESH = pl.DeviceIdType.MESH
BF = jnp.bfloat16
F32 = jnp.float32
ROUNDS = 4
STAGGER = 3
NT = (((1,), (1,)), ((), ()))


def kernel(NX, NY, NZ, per, BL, grad_h, eid_ref, sid_ref, prob_ref, tab_ref, w_h, hid_h,
           dh_ref, dp_ref,
           grad_v, w_v, hid_v, sendx, rx, swap, tok, wbuf, rets, retr, own, outs, res, wpad, perm,
           msgs, back,
           load_sem, yf_send, ring_send, ring_sem, sib_sem, xs_sem, xr_sem, sw_send, sw_recv,
           rt_send, rt_recv, out_send, out_recv, pb_send, pb_recv):
    NB = NY // 2
    NI = NY // 4
    CR = NI * 128 // NZ
    SL = 48
    C0 = NX * per
    CP = -(-(C0 + NX) // 16) * 16
    CA = -(-(CP // 2) // 16) * 16
    CELLS = NX * NY * per
    half = NZ // 2

    x = lax.axis_index("node")
    y = lax.axis_index("local")
    dp = lax.axis_index("dp")
    z = lax.div(dp, 2)
    k = lax.rem(dp, 2)
    par = lax.rem(y, 2)
    sib = {"dp": dp + 1 - 2 * k}
    z_up = {"dp": lax.rem(z + 1, NZ) * 2 + k}
    z_dn = {"dp": lax.rem(z + NZ - 1, NZ) * 2 + k}
    y_up = {"local": lax.rem(y + 1, NY)}
    y_dn = {"local": lax.rem(y + NY - 1, NY)}

    def remote(src, dst, ss, rs, dev):
        pltpu.make_async_remote_copy(src_ref=src, dst_ref=dst, send_sem=ss, recv_sem=rs,
                                     device_id=dev, device_id_type=MESH).start()

    def await_bytes(ref, sem):
        pltpu.make_async_copy(ref, ref, sem).wait()

    g_copy = pltpu.make_async_copy(grad_h, grad_v, load_sem.at[0])
    g_copy.start()
    w_copy = pltpu.make_async_copy(w_h, w_v, load_sem.at[1])
    w_copy.start()
    h_copy = pltpu.make_async_copy(hid_h, hid_v, load_sem.at[2])
    h_copy.start()

    bar = pltpu.get_barrier_semaphore()
    group = NX * NY
    mine = x * NY + y

    def greet(i, _):
        p = lax.rem(mine + i, group)
        pl.semaphore_signal(bar, inc=1, device_id={"node": lax.div(p, NY), "local": lax.rem(p, NY)},
                            device_id_type=MESH)
        return 0

    for dev in (z_up, z_dn, sib):
        pl.semaphore_signal(bar, inc=1, device_id=dev, device_id_type=MESH)
    lax.fori_loop(1, group, greet, 0)
    pl.semaphore_wait(bar, group - 1 + 3)

    for r in range(ROUNDS):
        at = z * CR
        row = (NB * k + 2 * lax.div(at, 128) + r % 2) * 256 + 128 * (r // 2) + lax.rem(at, 128)
        row = pl.multiple_of(row, 16)
        for j in range(1, NB):
            remote(w_h.at[pl.ds(row, CR)], wbuf.at[(r * 2 + k) * NZ + z, j - 1], yf_send,
                   ring_sem.at[r * NZ + z], {"local": lax.rem(y + NY - 2 * j, NY)})

    g_copy.wait()
    eid, sid = eid_ref[...], sid_ref[...]
    prow = jnp.broadcast_to(prob_ref[...], (16, prob_ref.shape[1])).astype(BF)
    T = eid.shape[1]
    rows_sl = lax.broadcasted_iota(jnp.int32, (SL, T), 0)
    rows_w = lax.broadcasted_iota(jnp.int32, (128, T), 0)
    rows_sl2 = lax.broadcasted_iota(jnp.int32, (SL, 128), 0)
    hot, wts = [], []
    for i in range(NX):
        e = lax.rem(x + i, NX)
        hot.append(jnp.where((eid == e) & (sid == rows_sl), 1.0, 0.0))
        hot_w = jnp.where((eid == e) & (sid == rows_w), 1.0, 0.0).astype(BF)
        wt = lax.dot_general(prow, hot_w, NT, preferred_element_type=F32)[0:1]
        wts.append(jnp.where(rows_sl2 == per, jnp.broadcast_to(wt, (SL, 128)), 0.0))
    hot = jnp.concatenate(hot, axis=0).astype(BF)
    wts = jnp.concatenate(wts, axis=0)
    for ph in range(2):
        pp = 1 - par if ph == 0 else par
        for jj in range(NB):
            b = 2 * jj + pp
            lanes = pl.ds(pl.multiple_of(b * BL, 128), BL)
            val = jnp.dot(hot, grad_v[:, lanes], preferred_element_type=F32)
            first = (val[:, 0:128] + wts).astype(BF)
            val = val.astype(BF)
            pj = pp * NB + jj
            for i in range(NX):
                cut = slice(SL * i, SL * (i + 1))
                if i == 0:
                    rx[pj, x] = val[cut]
                    rx[pj, x, :, 0:128] = first[cut]
                else:
                    sendx[i - 1, pj] = val[cut]
                    sendx[i - 1, pj, :, 0:128] = first[cut]
        for i in range(1, NX):
            remote(sendx.at[i - 1, pl.ds(pp * NB, NB)], rx.at[pl.ds(pp * NB, NB), x], xs_sem,
                   xr_sem.at[ph], {"node": lax.rem(x + i, NX)})

    def ring(r, d):
        base = (r * 2 + k) * NZ

        def chunk(src):
            await_bytes(wbuf.at[base + src], ring_sem.at[r * NZ + src])

        def pass_on(src, dev):
            remote(wbuf.at[base + src], wbuf.at[base + src], ring_send.at[r],
                   ring_sem.at[r * NZ + src], dev)

        def to_sibling(src):
            remote(wbuf.at[base + src], wbuf.at[base + src], ring_send.at[r], sib_sem.at[r], sib)

        d_up = half if r % 2 == 0 else half - 1
        d_dn = NZ - 1 - d_up
        if d == 0:
            chunk(z)
            if d_up > 0:
                pass_on(z, z_up)
            if d_dn > 0:
                pass_on(z, z_dn)
            to_sibling(z)
            return
        for up in (True, False):
            reach = d_up if up else d_dn
            if d > reach:
                continue
            src = lax.rem(z + NZ - d, NZ) if up else lax.rem(z + d, NZ)
            chunk(src)
            if d < reach:
                pass_on(src, z_up if up else z_dn)
            to_sibling(src)

    def compact(ph):
        q = lax.broadcasted_iota(jnp.int32, (CP, NX * SL), 0)
        c = lax.broadcasted_iota(jnp.int32, (CP, NX * SL), 1)
        keep = q < 0
        for n in range(NX):
            keep = keep | ((q >= per * n) & (q < per * (n + 1)) & (c - SL * n == q - per * n))
            keep = keep | ((q == C0 + n) & (c == SL * n + per))
        pick = jnp.where(keep, 1.0, 0.0).astype(BF)
        await_bytes(sendx.at[:, pl.ds(0, NB)], xr_sem.at[ph])
        pp = 1 - par if ph == 0 else par
        for j in range(NB):
            jj = j if ph == 0 else lax.div(lax.rem(y + 2 * j, NY), 2)
            got = rx[pp * NB + jj].reshape(NX * SL, BL)
            val = jnp.dot(pick, got, preferred_element_type=F32).astype(BF)
            if ph == 0:
                swap[jj] = val
            else:
                tok[j, 0:CP] = val
                if j == 0:
                    wpad[...] = val[:, 0:128]
        if ph == 0:
            for j in range(NB):
                lo = lax.div(lax.rem(y + NY - 1 + 2 * j, NY), 2)
                hi = lax.div(lax.rem(y + 1 + 2 * j, NY), 2)
                remote(swap.at[lo, pl.ds(0, CA)], tok.at[j, pl.ds(CP, CA)], sw_send, sw_recv, y_dn)
                remote(swap.at[hi, pl.ds(CA, CP - CA)], tok.at[j, pl.ds(CP + CA, CP - CA)],
                       sw_send, sw_recv, y_up)

    def compute(r):
        await_bytes(wbuf.at[pl.ds((r * 2 + 1 - k) * NZ, NZ)], sib_sem.at[r])
        for kk in range(2):
            own_w = [w_v[pl.ds((NB * kk + 2 * i + r % 2) * 256 + 128 * (r // 2), 128), :]
                     for i in range(NI)]
            own_w = jnp.concatenate(own_w, axis=0) if NI > 1 else own_w[0]
            acc = lax.dot_general(tok[0], own_w, NT, preferred_element_type=F32)
            for j in range(1, NB):
                wj = wbuf[(r * 2 + kk) * NZ:(r * 2 + kk + 1) * NZ, j - 1].reshape(NI * 128, BL)
                acc = acc + lax.dot_general(tok[j], wj, NT, preferred_element_type=F32)
            own[kk] = acc[0:CP]
            m = r * 2 + kk
            rets[m] = acc[CP:2 * CP].astype(BF)
            remote(rets.at[m, pl.ds(0, CA)], retr.at[m, pl.ds(0, CA)], rt_send, rt_recv.at[m], y_up)
            remote(rets.at[m, pl.ds(CA, CP - CA)], retr.at[m, pl.ds(CA, CP - CA)], rt_send,
                   rt_recv.at[m], y_dn)

    def finish(r):
        h = r // 2
        rows = lax.broadcasted_iota(jnp.int32, (CP, 128), 0)
        for kk in range(2):
            m = r * 2 + kk
            await_bytes(retr.at[m], rt_recv.at[m])
            for i in range(NI):
                cut = slice(128 * i, 128 * (i + 1))
                val = own[kk, :, cut] + retr[m, :, cut].astype(F32)
                val = jnp.where(rows >= C0, wpad[...].astype(F32), val).astype(BF)
                dest = NB * kk + 2 * i + r % 2
                slot = m * NI + i
                outs[slot] = val

                @pl.when(y != dest)
                def _():
                    remote(outs.at[slot], res.at[h * NY + y], out_send, out_recv.at[h],
                           {"local": jnp.int32(dest)})

                @pl.when(y == dest)
                def _():
                    res[h * NY + dest] = val

    def tail(h):
        await_bytes(res.at[pl.ds(0, NY - 1)], out_recv.at[h])
        got = res[h * NY:(h + 1) * NY]
        raw = lax.dot_general(got.reshape(NY * CP, 128), perm[...], (((0,), (0,)), ((), ())),
                              preferred_element_type=F32)
        s_row = tab_ref[2:3, :]
        spread = jnp.where(lax.broadcasted_iota(jnp.int32, (128, CELLS), 0) == s_row, 1.0, 0.0)
        last = C0 // 16 * 16
        sheet = got[:, last:last + 16, :].reshape(NY * 16, 128)
        wide = jnp.dot(sheet, spread.astype(BF), preferred_element_type=F32)
        mine_row = lax.broadcasted_iota(jnp.int32, (NY * 16, CELLS), 0)
        w_row = jnp.sum(jnp.where(mine_row == tab_ref[3:4, :], wide, 0.0), axis=0, keepdims=True)
        dh_ref[pl.ds(128 * h, 128), :] = (raw * w_row).astype(BF)
        saved = hid_v[pl.ds(128 * h, 128), :].astype(F32)
        return jnp.sum(saved * raw, axis=0, keepdims=True)

    def build_perm():
        for l in range(NY):
            q = lax.broadcasted_iota(jnp.int32, (CP, CELLS), 0) + l * CP
            perm[l * CP:(l + 1) * CP, :] = jnp.where(q == tab_ref[0:1, :], 1.0, 0.0).astype(BF)

    last_t = half + STAGGER * (ROUNDS - 1)
    route = None
    for t in range(last_t + 1):
        for r in range(ROUNDS):
            if 0 <= t - STAGGER * r <= half:
                ring(r, t - STAGGER * r)
        if t == min(1, last_t):
            build_perm()
            w_copy.wait()
            h_copy.wait()
        if t == half // 2:
            compact(0)
        if t == half - 1:
            compact(1)
        if t == half:
            await_bytes(tok.at[:, pl.ds(CP, CP)], sw_recv)
        for r in range(ROUNDS):
            done = half + STAGGER * r
            if t == done:
                compute(r)
                if r == ROUNDS - 1:
                    finish(r)
            elif t == done + 1:
                finish(r)
    route = tail(0) + tail(1)

    src_rows = lax.broadcasted_iota(jnp.int32, (group, CELLS), 0)
    split = jnp.where(src_rows == tab_ref[1:2, :], jnp.broadcast_to(route, (group, CELLS)), 0.0)
    spread = jnp.where(lax.broadcasted_iota(jnp.int32, (128, CELLS), 0) == tab_ref[2:3, :], 1.0, 0.0)
    rows = lax.dot_general(split, spread, NT, preferred_element_type=F32,
                           precision=lax.Precision.HIGHEST)
    msgs[...] = jnp.broadcast_to(rows[:, None, :], (group, 8, 128))
    back[mine] = msgs[mine]

    def give(i, _):
        p = lax.rem(mine + i, group)
        remote(msgs.at[p], back.at[mine], pb_send, pb_recv,
               {"node": lax.div(p, NY), "local": lax.rem(p, NY)})
        return 0

    lax.fori_loop(1, group, give, 0)
    await_bytes(back.at[pl.ds(0, group - 1)], pb_recv)
    sums = [jnp.sum(back[e * NY:(e + 1) * NY], axis=0)[0:1] for e in range(NX)]
    slot_hot = jnp.where(sid == rows_w, 1.0, 0.0)
    total = jnp.zeros((8, T), F32)
    for e in range(NX):
        got = jnp.dot(jnp.broadcast_to(sums[e], (8, 128)), slot_hot, preferred_element_type=F32,
                      precision=lax.Precision.HIGHEST)
        total = total + jnp.where(eid == e, got, 0.0)
    dp_ref[...] = total

    await_bytes(wbuf.at[pl.ds(0, ROUNDS * (NB - 1)), 0], yf_send)
    for r in range(ROUNDS):
        await_bytes(wbuf.at[pl.ds(0, 2 * NZ - 1)], ring_send.at[r])
    await_bytes(sendx, xs_sem)
    await_bytes(tok.at[:, pl.ds(CP, CP)], sw_send)
    await_bytes(rets, rt_send)
    await_bytes(outs.at[pl.ds(0, 2 * (NY - 1))], out_send)
    await_bytes(back.at[pl.ds(0, group - 1)], pb_send)


def body(NX, NY, NZ, grad_out, probs, expert_ids, slot_ids, w_down, hidden):
    T, D = grad_out.shape
    ff, BL = w_down.shape[1:]
    cells = hidden.shape[2]
    group = NX * NY
    per = cells // group
    NB, NI = NY // 2, NY // 4
    C0 = NX * per
    CP = -(-(C0 + NX) // 16) * 16
    cell = np.arange(cells)
    src, s = cell // per, cell % per
    n, l = src // NY, src % NY
    tab = np.zeros((8, cells), np.int32)
    tab[0] = l * CP + n * per + s
    tab[1] = src
    tab[2] = s
    tab[3] = l * 16 + C0 % 16 + n
    vm = pl.BlockSpec(memory_space=pltpu.VMEM)
    anym = pl.BlockSpec(memory_space=pl.ANY)
    V, DMA = pltpu.VMEM, pltpu.SemaphoreType.DMA
    dh, dpr = pl.pallas_call(
        functools.partial(kernel, NX, NY, NZ, per, BL),
        out_shape=(jax.ShapeDtypeStruct((ff // NY, cells), BF), jax.ShapeDtypeStruct((8, T), F32)),
        in_specs=[anym, vm, vm, vm, vm, anym, anym],
        out_specs=(vm, vm),
        scratch_shapes=[
            V((T, D), BF), V((ff, BL), BF), V((ff // NY, cells), BF),
            V((NX - 1, NY, 48, BL), BF), V((NY, NX, 48, BL), BF),
            V((NB, CP, BL), BF), V((NB, 2 * CP, BL), BF),
            V((ROUNDS * 2 * NZ, NB - 1, NI * 128 // NZ, BL), BF),
            V((2 * ROUNDS, CP, NI * 128), BF), V((2 * ROUNDS, CP, NI * 128), BF),
            V((2, CP, NI * 128), F32), V((2 * ROUNDS * NI, CP, 128), BF),
            V((2 * NY, CP, 128), BF), V((CP, 128), BF), V((NY * CP, cells), BF),
            V((group, 8, 128), F32), V((group, 8, 128), F32),
            DMA((3,)), DMA, DMA((ROUNDS,)), DMA((ROUNDS * NZ,)), DMA((ROUNDS,)), DMA, DMA((2,)),
            DMA, DMA, DMA, DMA((2 * ROUNDS,)), DMA, DMA((2,)), DMA, DMA,
        ],
        compiler_params=pltpu.CompilerParams(
            collective_id=0, has_side_effects=True, vmem_limit_bytes=58 * 1024 * 1024),
        cost_estimate=pl.CostEstimate(flops=2 * ff * cells * BL, bytes_accessed=8 << 20,
                                      transcendentals=0),
    )(grad_out, expert_ids.reshape(1, T), slot_ids.reshape(1, T), probs.reshape(1, T),
      jnp.asarray(tab), w_down[0], hidden[0])
    return dh[None], dpr[0]


def solution(mesh):
    NX, NY, NZ = mesh.shape["node"], mesh.shape["local"], mesh.shape["dp"] // 2
    return jax.shard_map(
        functools.partial(body, NX, NY, NZ),
        mesh=mesh,
        in_specs=(
            P(("dp", "node", "local"), None),
            P(("dp", "node", "local")),
            P(("dp", "node", "local")),
            P(("dp", "node", "local")),
            P("node", None, "local"),
            P(("dp", "node"), "local", None),
        ),
        out_specs=(P(("dp", "node"), "local", None), P(("dp", "node", "local"))),
        check_vma=False,
    )
```

time: 197 us -> 140 us (0.71)
  Pallas kernels: 0 us -> 133 us
  blocking collectives: 73.5 us -> 0 us
  waiting for transfers between devices: 61.7 us -> 0 us
  local copies, waits for them, and re-layouts: 27.9 us -> 5.38 us
  between operations: 14.1 us -> 0.64 us
  matrix products: 10.3 us -> 0 us
  starting transfers between devices: 7.04 us -> 0 us
  other arithmetic: 2.25 us -> 0 us
    pallas_call x0 -> x1, Pallas kernels: none -> 133 us  [body(): pl.pallas_call(functools.partial(kernel, NX, NY, NZ, per, BL), out_shape=...]
    all_to_all x2 -> x0, blocking collectives: 73.5 us -> none  [the longest x1 58 us: body(): lax.all_to_all(send_rows.reshape(sources, per_source, piece), ('node', 'l...]
    reduce_scatter x1 -> x0, waiting for transfers between devices: 53 us -> none  [body(): lax.psum_scatter(lax.dot_general(weight_local, received, (((1,), (1,)), (...]
    scatter x4 -> x0, local copies, waits for them, and re-layouts: 20.3 us -> none  [the longest x2 13.3 us: body(): send_rows = jnp.zeros((n_node, n_local, per_source, piece), jnp.bfloat16)...]
    dot_general x2 -> x0, matrix products: 10.3 us -> none  [the longest x1 9.48 us: body(): lax.dot_general(weight_local, received, (((1,), (1,)), ((), ())), preferr...]
    all_to_all x1 -> x0, waiting for transfers between devices: 8.61 us -> none  [body(): lax.all_to_all(route_part.reshape(sources, per_source), ('node', 'local')...]
    all_to_all x1 -> x0, starting transfers between devices: 7 us -> none  [body(): lax.all_to_all(route_part.reshape(sources, per_source), ('node', 'local')...]
    reshape x3 -> x0, local copies, waits for them, and re-layouts: 2.78 us -> none  [the longest x1 2.04 us: body(): received = got_rows.reshape(cells, piece)]
  transfers between devices with their start and end apart: 2 -> 0, of which waited for: 2 -> 0; matrix products, arithmetic and copies ran while one was open for 4% -> 0% of each run, Pallas kernels for 0% -> 0%
where the time goes in v1:
time: 140 us; the launch traced here: 139 us
  Pallas kernels  133 us (95%)
  local copies, waits for them, and re-layouts  5.38 us (4%)
    pallas_call x1, Pallas kernels, body(): pl.pallas_call(functools.partial(kernel, NX, NY, NZ, per, BL), out_shape=...  133 us
    unnamed x2, local copies, waits for them, and re-layouts  4.2 us

profile of v1, /device:TPU:1, one launch (start us, length us, event | category | flops | bytes accessed | tf_op | source)
XLA Modules:
  0.0 139.2 jit_solution(8677497985745111751)
XLA Ops:
  0.6 2.1 %copy.9 = bf16[1,256,1088]{2,1,0:T(8,128)(2,1)} copy(bf16[1,256,1088]{1,2,0:T(8,128)(2,1)} %param.12) | data formatting | bytes 1114112 | tf_op args[5]
  2.7 133.2 %shard_map.86 = (bf16[256,1088]{1,0:T(8,128)(2,1)}, f32[8,128]{1,0:T(8,128)}) custom-call(bf16[128,7168]{1,0:T(8,128)(2,1)} %grad_h.1, s32[1,128]{1,0:T(1,128)} %bitcast.11, s32[1,128]{1,0:T(1,128)} %bitcast.12, f32[1,128]{1,0:T(1,128)} %bitcast.13, s32[8,1088]{1,0:T(8,128)} %constant.2.clone.tab_ref, bf16[2048,896]{1,0:T(8,128)(2,1)} %bitcast.10, ...), custom_call_target="tpu_custom_call" | custom-call | flops 3992977408 | bytes 8388608 | tf_op jit(solution)/shard_map/pallas_call | solution.py:324
  136.0 2.1 %copy.10 = bf16[1,256,1088]{1,2,0:T(8,128)(2,1)} copy(bf16[1,256,1088]{2,1,0:T(8,128)(2,1)} %bitcast.8) | data formatting | bytes 1114112
  138.1 1.2 slice_bitcast_fusion

commit v2 on v1

v2 whole, which is shorter than its diff:
```python
import contextlib
import functools

import jax
import jax.numpy as jnp
from jax import lax
from jax.experimental import pallas as pl
from jax.experimental.pallas import tpu as pltpu
from jax.sharding import PartitionSpec as P

MESH = pl.DeviceIdType.MESH
BF = jnp.bfloat16
F32 = jnp.float32
ROUNDS = 4
STAGGER = 2
DIRECT = (2, 2, 2, 2)
COMPACT = (4, 6)
NT = (((1,), (1,)), ((), ()))


def stage(_):
    return contextlib.nullcontext()


def kernel(NX, NY, NZ, per, BL, grad_h, eid_ref, sid_ref, prob_ref, w_h, hid_h,
           dh_ref, dp_ref,
           grad_v, w_v, hid_v, sendx, rx, swap, tok, wbuf, rets, retr, own, outs, res, wpad, perm,
           wcol, zacc, msgs, back,
           load_sem, yf_send, ring_send, ring_sem, sib_sem, xs_sem, xr_sem, sw_send, sw_recv,
           rt_send, rt_recv, out_send, out_recv, pb_send, pb_recv):
    NB = NY // 2
    NI = NY // 4
    CR = NI * 128 // NZ
    SL = 48
    C0 = NX * per
    CP = -(-(C0 + NX) // 16) * 16
    CA = -(-(CP // 2) // 16) * 16
    CELLS = NX * NY * per

    x = lax.axis_index("node")
    y = lax.axis_index("local")
    dp = lax.axis_index("dp")
    z = lax.div(dp, 2)
    k = lax.rem(dp, 2)
    par = lax.rem(y, 2)
    sib = {"dp": dp + 1 - 2 * k}
    z_up = {"dp": lax.rem(z + 1, NZ) * 2 + k}
    z_dn = {"dp": lax.rem(z + NZ - 1, NZ) * 2 + k}
    y_up = {"local": lax.rem(y + 1, NY)}
    y_dn = {"local": lax.rem(y + NY - 1, NY)}

    def remote(src, dst, ss, rs, dev):
        pltpu.make_async_remote_copy(src_ref=src, dst_ref=dst, send_sem=ss, recv_sem=rs,
                                     device_id=dev, device_id_type=MESH).start()

    def await_bytes(ref, sem):
        pltpu.make_async_copy(ref, ref, sem).wait()

    g_copy = pltpu.make_async_copy(grad_h, grad_v, load_sem.at[0])
    g_copy.start()
    w_copy = pltpu.make_async_copy(w_h, w_v, load_sem.at[1])
    w_copy.start()
    h_copy = pltpu.make_async_copy(hid_h, hid_v, load_sem.at[2])
    h_copy.start()

    bar = pltpu.get_barrier_semaphore()
    group = NX * NY
    mine = x * NY + y

    def greet(i, _):
        p = lax.rem(mine + i, group)
        pl.semaphore_signal(bar, inc=1, device_id={"node": lax.div(p, NY), "local": lax.rem(p, NY)},
                            device_id_type=MESH)
        return 0

    for dev in (z_up, z_dn, sib):
        pl.semaphore_signal(bar, inc=1, device_id=dev, device_id_type=MESH)
    lax.fori_loop(1, group, greet, 0)
    pl.semaphore_wait(bar, group - 1 + 3)

    def share(r, plane):
        at = plane * CR
        row = (NB * k + 2 * lax.div(at, 128) + r % 2) * 256 + 128 * (r // 2) + lax.rem(at, 128)
        row = pl.multiple_of(row, 16)
        for j in range(1, NB):
            remote(w_h.at[pl.ds(row, CR)], wbuf.at[(r * 2 + k) * NZ + plane, j - 1], yf_send,
                   ring_sem.at[(r * NZ + plane) * (NB - 1) + j - 1],
                   {"local": lax.rem(y + NY - 2 * j, NY)})

    count = [min(DIRECT[r], NZ - 1) for r in range(ROUNDS)]
    up = [(NZ - 1 - count[r] + (r % 2 == 0)) // 2 for r in range(ROUNDS)]
    down = [NZ - 1 - count[r] - up[r] for r in range(ROUNDS)]
    last = [max(up[r], down[r]) for r in range(ROUNDS)]

    def direct(r):
        return [lax.rem(z + down[r] + 1 + i, NZ) for i in range(count[r])]

    share(0, z)
    share(1, z)

    g_copy.wait()
    eid, sid = eid_ref[...], sid_ref[...]
    prow = jnp.broadcast_to(prob_ref[...], (16, prob_ref.shape[1])).astype(BF)
    T = eid.shape[1]
    rows_sl = lax.broadcasted_iota(jnp.int32, (SL, T), 0)
    rows_w = lax.broadcasted_iota(jnp.int32, (128, T), 0)
    rows_sl2 = lax.broadcasted_iota(jnp.int32, (SL, 128), 0)
    hot, wts = [], []
    for i in range(NX):
        e = lax.rem(x + i, NX)
        hot.append(jnp.where((eid == e) & (sid == rows_sl), 1.0, 0.0))
        hot_w = jnp.where((eid == e) & (sid == rows_w), 1.0, 0.0).astype(BF)
        wt = lax.dot_general(prow, hot_w, NT, preferred_element_type=F32)[0:1]
        wts.append(jnp.where(rows_sl2 == per, jnp.broadcast_to(wt, (SL, 128)), 0.0))
    hot = jnp.concatenate(hot, axis=0).astype(BF)
    wts = jnp.concatenate(wts, axis=0)
    def pack(ph):
        pp = 1 - par if ph == 0 else par
        for jj in range(NB):
            b = 2 * jj + pp
            lanes = pl.ds(pl.multiple_of(b * BL, 128), BL)
            val = jnp.dot(hot, grad_v[:, lanes], preferred_element_type=F32)
            first = (val[:, 0:128] + wts).astype(BF)
            val = val.astype(BF)
            pj = pp * NB + jj
            for i in range(NX):
                cut = slice(SL * i, SL * (i + 1))
                if i == 0:
                    rx[pj, x] = val[cut]
                    rx[pj, x, :, 0:128] = first[cut]
                else:
                    sendx[i - 1, pj] = val[cut]
                    sendx[i - 1, pj, :, 0:128] = first[cut]
        for i in range(1, NX):
            remote(sendx.at[i - 1, pl.ds(pp * NB, NB)], rx.at[pl.ds(pp * NB, NB), x], xs_sem,
                   xr_sem.at[ph], {"node": lax.rem(x + i, NX)})

    def ring(r, d):
        base = (r * 2 + k) * NZ

        def chunk(src, j):
            await_bytes(wbuf.at[base + src, j], ring_sem.at[(r * NZ + src) * (NB - 1) + j])

        def pass_on(src, j, dev):
            remote(wbuf.at[base + src, j], wbuf.at[base + src, j], ring_send.at[r],
                   ring_sem.at[(r * NZ + src) * (NB - 1) + j], dev)

        def to_sibling(src):
            remote(wbuf.at[base + src], wbuf.at[base + src], ring_send.at[r], sib_sem.at[r], sib)

        moves = []
        if d == 0:
            moves.append((z, [z_up] * (up[r] > 0) + [z_dn] * (down[r] > 0)))
        if 0 < d <= up[r]:
            moves.append((lax.rem(z + NZ - d, NZ), [z_up] if d < up[r] else []))
        if 0 < d <= down[r]:
            moves.append((lax.rem(z + d, NZ), [z_dn] if d < down[r] else []))
        if d == last[r]:
            moves.extend((plane, []) for plane in direct(r))
        for j in range(NB - 1):
            for src, devs in moves:
                chunk(src, j)
                for dev in devs:
                    pass_on(src, j, dev)
        for src, _ in moves:
            to_sibling(src)

    def compact(ph):
        q = lax.broadcasted_iota(jnp.int32, (CP, NX * SL), 0)
        c = lax.broadcasted_iota(jnp.int32, (CP, NX * SL), 1)
        keep = q < 0
        for n in range(NX):
            keep = keep | ((q >= per * n) & (q < per * (n + 1)) & (c - SL * n == q - per * n))
            keep = keep | ((q == C0 + n) & (c == SL * n + per))
        pick = jnp.where(keep, 1.0, 0.0).astype(BF)
        await_bytes(sendx.at[:, pl.ds(0, NB)], xr_sem.at[ph])
        pp = 1 - par if ph == 0 else par
        for j in range(NB):
            jj = j if ph == 0 else lax.div(lax.rem(y + 2 * j, NY), 2)
            got = rx[pp * NB + jj].reshape(NX * SL, BL)
            val = jnp.dot(pick, got, preferred_element_type=F32).astype(BF)
            if ph == 0:
                swap[jj] = val
            else:
                tok[j, 0:CP] = val
                if j == 0:
                    wpad[...] = val[:, 0:128]
        if ph == 0:
            for j in range(NB):
                lo = lax.div(lax.rem(y + NY - 1 + 2 * j, NY), 2)
                hi = lax.div(lax.rem(y + 1 + 2 * j, NY), 2)
                remote(swap.at[lo, pl.ds(0, CA)], tok.at[j, pl.ds(CP, CA)], sw_send, sw_recv, y_dn)
                remote(swap.at[hi, pl.ds(CA, CP - CA)], tok.at[j, pl.ds(CP + CA, CP - CA)],
                       sw_send, sw_recv, y_up)

    def compute(r, step):
        if step == 1:
            await_bytes(wbuf.at[pl.ds((r * 2 + 1 - k) * NZ, NZ)], sib_sem.at[r])
        kk = k if step == 0 else 1 - k
        own_w = [w_v[pl.ds(pl.multiple_of(
            (NB * kk + 2 * i + r % 2) * 256 + 128 * (r // 2), 128), 128), :] for i in range(NI)]
        own_w = jnp.concatenate(own_w, axis=0) if NI > 1 else own_w[0]
        acc = lax.dot_general(tok[0], own_w, NT, preferred_element_type=F32)
        for j in range(1, NB):
            wj = wbuf[pl.ds((r * 2 + kk) * NZ, NZ), j - 1].reshape(NI * 128, BL)
            acc = acc + lax.dot_general(tok[j], wj, NT, preferred_element_type=F32)
        m = r * 2 + step
        rets[m] = acc[CP:2 * CP].astype(BF)
        remote(rets.at[m, pl.ds(0, CA)], retr.at[m, pl.ds(0, CA)], rt_send, rt_recv.at[m], y_up)
        remote(rets.at[m, pl.ds(CA, CP - CA)], retr.at[m, pl.ds(CA, CP - CA)], rt_send,
               rt_recv.at[m], y_dn)
        own[step] = acc[0:CP]

    def finish(r, step):
        h = r // 2
        kk = k if step == 0 else 1 - k
        rows = lax.broadcasted_iota(jnp.int32, (CP, 128), 0)
        m = r * 2 + step
        await_bytes(retr.at[m], rt_recv.at[m])
        for i in range(NI):
            cut = slice(128 * i, 128 * (i + 1))
            val = own[step, :, cut] + retr[m, :, cut].astype(F32)
            val = jnp.where(rows >= C0, wpad[...].astype(F32), val).astype(BF)
            dest = NB * kk + 2 * i + r % 2
            slot = m * NI + i
            outs[slot] = val

            @pl.when(y != dest)
            def _():
                remote(outs.at[slot], res.at[h * NY + y], out_send, out_recv.at[h],
                       {"local": dest})

            @pl.when(y == dest)
            def _():
                res[h * NY + dest] = val

    def cell_parts(rows, lanes, dim):
        c = lax.broadcasted_iota(jnp.int32, (rows, lanes), dim).astype(F32)
        src = jnp.floor((c + 0.5) / per)
        n = jnp.floor((src + 0.5) / NY)
        return (v.astype(jnp.int32) for v in (src, c - per * src, n, src - NY * n))

    def build_perm():
        _, s, n, l = cell_parts(CELLS, 128, 0)
        at = l * CP + n * per + s
        for lo in range(0, NY * CP, 128):
            width = min(128, NY * CP - lo)
            q = lax.broadcasted_iota(jnp.int32, (CELLS, width), 1) + lo
            perm[:, lo:lo + width] = jnp.where(q == at[:, :width], 1.0, 0.0).astype(BF)

    def tail(h):
        await_bytes(res.at[pl.ds(0, NY - 1)], out_recv.at[h])
        got = res[h * NY:(h + 1) * NY]
        raw = jnp.dot(perm[...], got.reshape(NY * CP, 128), preferred_element_type=F32)
        if h == 0:
            _, s, n, l = cell_parts(CELLS, 128, 0)
            last = C0 // 16 * 16
            sheet = got[:, last:last + 16, :].reshape(NY * 16, 128)
            at = (l * 16 + C0 % 16 + n)[:, :NY * 16]
            q = lax.broadcasted_iota(jnp.int32, (CELLS, NY * 16), 1)
            wide = jnp.dot(jnp.where(q == at, 1.0, 0.0).astype(BF), sheet, preferred_element_type=F32)
            lane = lax.broadcasted_iota(jnp.int32, (CELLS, 128), 1)
            one = jnp.sum(jnp.where(lane == s, wide, 0.0), axis=1, keepdims=True)
            wcol[...] = jnp.broadcast_to(one, (CELLS, 128))
        cut = slice(128 * h, 128 * (h + 1))
        dh_ref[:, cut] = (raw * wcol[...]).astype(BF)
        part = hid_v[:, cut].astype(F32) * raw
        if h == 0:
            zacc[...] = part
        else:
            zacc[...] = zacc[...] + part

    with stage("pack0"):
        pack(0)
    done = [last[r] + STAGGER * r for r in range(ROUNDS)]
    for t in range(max(done) + 1):
        for r in range(ROUNDS):
            if 0 <= t - STAGGER * r <= last[r]:
                with stage(f"ring{r}_{t - STAGGER * r}"):
                    ring(r, t - STAGGER * r)
        if t == 0:
            share(2, z)
            share(3, z)
            with stage("pack1"):
                pack(1)
            for r in range(ROUNDS):
                share(r, direct(r)[0])
        if t == min(1, last[0] - 1):
            with stage("perm"):
                build_perm()
                w_copy.wait()
                h_copy.wait()
            for r in range(ROUNDS):
                for plane in direct(r)[1:]:
                    share(r, plane)
        if t == min(COMPACT[0], last[0]):
            with stage("compact0"):
                compact(0)
        if t == min(COMPACT[1], last[0]):
            with stage("compact1"):
                compact(1)
        if t == done[0]:
            with stage("swapwait"):
                await_bytes(tok.at[:, pl.ds(CP, CP)], sw_recv)
        for r in range(ROUNDS):
            if t == done[r] + 1:
                with stage(f"finish{r}"):
                    finish(r, 0)
                    finish(r, 1)
        for r in range(ROUNDS):
            if t == done[r]:
                with stage(f"compute{r}"):
                    compute(r, 0)
                    compute(r, 1)
    finish(ROUNDS - 1, 0)
    with stage("tail0"):
        tail(0)
    finish(ROUNDS - 1, 1)
    with stage("tail1"):
        tail(1)

    _, s, _, _ = cell_parts(CELLS, 128, 0)
    lane = lax.broadcasted_iota(jnp.int32, (CELLS, 128), 1)
    spread = jnp.where(lane == s, jnp.sum(zacc[...], axis=1, keepdims=True), 0.0)
    src, _, _, _ = cell_parts(group, CELLS, 1)
    pick = jnp.where(src == lax.broadcasted_iota(jnp.int32, (group, CELLS), 0), 1.0, 0.0)
    rows = jnp.dot(pick, spread, preferred_element_type=F32, precision=lax.Precision.HIGHEST)
    msgs[...] = jnp.broadcast_to(rows[:, None, :], (group, 8, 128))
    back[mine] = msgs[mine]

    def give(i, _):
        p = lax.rem(mine + i, group)
        remote(msgs.at[p], back.at[mine], pb_send, pb_recv,
               {"node": lax.div(p, NY), "local": lax.rem(p, NY)})
        return 0

    lax.fori_loop(1, group, give, 0)
    await_bytes(back.at[pl.ds(0, group - 1)], pb_recv)
    sums = jnp.concatenate(
        [jnp.sum(back[e * NY:(e + 1) * NY], axis=0)[0:1] for e in range(NX)]
        + [jnp.zeros((8 - NX, 128), F32)], axis=0)
    slot_hot = jnp.where(sid == rows_w, 1.0, 0.0)
    got = jnp.dot(sums, slot_hot, preferred_element_type=F32, precision=lax.Precision.HIGHEST)
    total = jnp.sum(jnp.where(eid == lax.broadcasted_iota(jnp.int32, (8, T), 0), got, 0.0),
                    axis=0, keepdims=True)
    dp_ref[...] = total

    await_bytes(wbuf.at[pl.ds(0, ROUNDS + sum(count))], yf_send)
    for r in range(ROUNDS):
        await_bytes(wbuf.at[pl.ds(0, NZ + up[r] + down[r])], ring_send.at[r])
    await_bytes(sendx, xs_sem)
    await_bytes(tok.at[:, pl.ds(CP, CP)], sw_send)
    await_bytes(rets, rt_send)
    await_bytes(outs.at[pl.ds(0, 2 * (NY - 1))], out_send)
    await_bytes(back.at[pl.ds(0, group - 1)], pb_send)


def body(NX, NY, NZ, grad_out, probs, expert_ids, slot_ids, w_down, hidden):
    T, D = grad_out.shape
    ff, BL = w_down.shape[1:]
    cells = hidden.shape[2]
    group = NX * NY
    per = cells // group
    NB, NI = NY // 2, NY // 4
    C0 = NX * per
    CP = -(-(C0 + NX) // 16) * 16
    vm = pl.BlockSpec(memory_space=pltpu.VMEM)
    anym = pl.BlockSpec(memory_space=pl.ANY)
    V, DMA = pltpu.VMEM, pltpu.SemaphoreType.DMA
    dh, dpr = pl.pallas_call(
        functools.partial(kernel, NX, NY, NZ, per, BL),
        out_shape=(jax.ShapeDtypeStruct((cells, ff // NY), BF), jax.ShapeDtypeStruct((1, T), F32)),
        in_specs=[anym, vm, vm, vm, anym, anym],
        out_specs=(vm, vm),
        scratch_shapes=[
            V((T, D), BF), V((ff, BL), BF), V((cells, ff // NY), BF),
            V((NX - 1, NY, 48, BL), BF), V((NY, NX, 48, BL), BF),
            V((NB, CP, BL), BF), V((NB, 2 * CP, BL), BF),
            V((ROUNDS * 2 * NZ, NB - 1, NI * 128 // NZ, BL), BF),
            V((2 * ROUNDS, CP, NI * 128), BF), V((2 * ROUNDS, CP, NI * 128), BF),
            V((2, CP, NI * 128), F32), V((2 * ROUNDS * NI, CP, 128), BF),
            V((2 * NY, CP, 128), BF), V((CP, 128), BF), V((cells, NY * CP), BF),
            V((cells, 128), F32), V((cells, 128), F32),
            V((group, 8, 128), F32), V((group, 8, 128), F32),
            DMA((3,)), DMA, DMA((ROUNDS,)), DMA((ROUNDS * NZ * (NB - 1),)), DMA((ROUNDS,)), DMA, DMA((2,)),
            DMA, DMA, DMA, DMA((2 * ROUNDS,)), DMA, DMA((2,)), DMA, DMA,
        ],
        compiler_params=pltpu.CompilerParams(
            collective_id=0, has_side_effects=True, vmem_limit_bytes=58 * 1024 * 1024),
        cost_estimate=pl.CostEstimate(flops=2 * ff * cells * BL, bytes_accessed=8 << 20,
                                      transcendentals=0),
    )(grad_out, expert_ids.reshape(1, T), slot_ids.reshape(1, T), probs.reshape(1, T),
      w_down[0], hidden[0].T)
    return dh.T[None], dpr[0]


def solution(mesh):
    NX, NY, NZ = mesh.shape["node"], mesh.shape["local"], mesh.shape["dp"] // 2
    return jax.shard_map(
        functools.partial(body, NX, NY, NZ),
        mesh=mesh,
        in_specs=(
            P(("dp", "node", "local"), None),
            P(("dp", "node", "local")),
            P(("dp", "node", "local")),
            P(("dp", "node", "local")),
            P("node", None, "local"),
            P(("dp", "node"), "local", None),
        ),
        out_specs=(P(("dp", "node"), "local", None), P(("dp", "node", "local"))),
        check_vma=False,
    )
```

time: 140 us -> 120 us (0.86)
  Pallas kernels: 133 us -> 116 us
  local copies, waits for them, and re-layouts: 5.38 us -> 3.04 us
    pallas_call x1, Pallas kernels: 133 us -> 116 us  [body(): pl.pallas_call(functools.partial(kernel, NX, NY, NZ, per, BL), out_shape=...]
where the time goes in v2:
time: 120 us
  Pallas kernels  116 us (97%)
  local copies, waits for them, and re-layouts  3.04 us (3%)
    pallas_call x1, Pallas kernels, body(): pl.pallas_call(functools.partial(kernel, NX, NY, NZ, per, BL), out_shape=...  116 us
    unnamed x2, local copies, waits for them, and re-layouts  3.04 us

profile of v2, /device:TPU:1, one launch (start us, length us, event | category | flops | bytes accessed | tf_op | source)
XLA Modules:
  0.0 119.8 jit_solution(12299746054051639092)
XLA Ops:
  0.6 116.1 %shard_map.77 = (bf16[1088,256]{1,0:T(8,128)(2,1)}, f32[1,128]{1,0:T(1,128)}) custom-call(bf16[128,7168]{1,0:T(8,128)(2,1)} %grad_h.1, s32[1,128]{1,0:T(1,128)} %bitcast.14, s32[1,128]{1,0:T(1,128)} %bitcast.15, f32[1,128]{1,0:T(1,128)} %bitcast.16, bf16[2048,896]{1,0:T(8,128)(2,1)} %bitcast.12, bf16[1088,256]{1,0:T(8,128)(2,1)} %bitcast.13), custom_call_target="tpu_custom_call" | custom-call | flops 3992977408 | bytes 8388608 | tf_op jit(solution)/shard_map/pallas_call | solution.py:370
  116.8 1.9 %copy.10 = bf16[1,256,1088]{1,2,0:T(8,128)(2,1)} copy(bf16[1,256,1088]{1,2,0:T(8,128)(2,1)} %bitcast.11) | data formatting | bytes 1114112
  118.7 1.1 copy.11

commit v3 on v2

--- a/solution.py
+++ b/solution.py
@@ -12,7 +12,7 @@
 BF = jnp.bfloat16
 F32 = jnp.float32
 ROUNDS = 4
-STAGGER = 2
+START = (0, 1, 3, 5)
 DIRECT = (2, 2, 2, 2)
 COMPACT = (4, 6)
 NT = (((1,), (1,)), ((), ()))
@@ -75,7 +75,8 @@
 
     for dev in (z_up, z_dn, sib):
         pl.semaphore_signal(bar, inc=1, device_id=dev, device_id_type=MESH)
-    lax.fori_loop(1, group, greet, 0)
+    for i in range(1, group):
+        greet(i, 0)
     pl.semaphore_wait(bar, group - 1 + 3)
 
     def share(r, plane):
@@ -272,24 +273,26 @@
 
     with stage("pack0"):
         pack(0)
-    done = [last[r] + STAGGER * r for r in range(ROUNDS)]
+    done = [last[r] + START[r] for r in range(ROUNDS)]
     for t in range(max(done) + 1):
         for r in range(ROUNDS):
-            if 0 <= t - STAGGER * r <= last[r]:
-                with stage(f"ring{r}_{t - STAGGER * r}"):
-                    ring(r, t - STAGGER * r)
+            if 0 <= t - START[r] <= last[r]:
+                with stage(f"ring{r}_{t - START[r]}"):
+                    ring(r, t - START[r])
         if t == 0:
             share(2, z)
             share(3, z)
+            for r in range(ROUNDS):
+                share(r, direct(r)[0])
+        if t == min(2, last[0] - 1):
             with stage("pack1"):
                 pack(1)
-            for r in range(ROUNDS):
-                share(r, direct(r)[0])
-        if t == min(1, last[0] - 1):
+        if t == min(5, last[0] - 1):
             with stage("perm"):
                 build_perm()
                 w_copy.wait()
                 h_copy.wait()
+        if t == min(1, last[0] - 1):
             for r in range(ROUNDS):
                 for plane in direct(r)[1:]:
                     share(r, plane)
@@ -334,7 +337,8 @@
                {"node": lax.div(p, NY), "local": lax.rem(p, NY)})
         return 0
 
-    lax.fori_loop(1, group, give, 0)
+    for i in range(1, group):
+        give(i, 0)
     await_bytes(back.at[pl.ds(0, group - 1)], pb_recv)
     sums = jnp.concatenate(
         [jnp.sum(back[e * NY:(e + 1) * NY], axis=0)[0:1] for e in range(NX)]

time: 120 us -> 117 us (0.975)
  Pallas kernels: 116 us -> 113 us
    pallas_call x1, Pallas kernels: 116 us -> 113 us  [body(): pl.pallas_call(functools.partial(kernel, NX, NY, NZ, per, BL), out_shape=...]
where the time goes in v3:
time: 117 us
  Pallas kernels  113 us (97%)
  local copies, waits for them, and re-layouts  3.04 us (3%)
    pallas_call x1, Pallas kernels, body(): pl.pallas_call(functools.partial(kernel, NX, NY, NZ, per, BL), out_shape=...  113 us
    unnamed x2, local copies, waits for them, and re-layouts  3.04 us

profile of v3, /device:TPU:1, one launch (start us, length us, event | category | flops | bytes accessed | tf_op | source)
XLA Modules:
  0.0 116.9 jit_solution(14921407460034050162)
XLA Ops:
  0.6 113.2 %shard_map.77 = (bf16[1088,256]{1,0:T(8,128)(2,1)}, f32[1,128]{1,0:T(1,128)}) custom-call(bf16[128,7168]{1,0:T(8,128)(2,1)} %grad_h.1, s32[1,128]{1,0:T(1,128)} %bitcast.14, s32[1,128]{1,0:T(1,128)} %bitcast.15, f32[1,128]{1,0:T(1,128)} %bitcast.16, bf16[2048,896]{1,0:T(8,128)(2,1)} %bitcast.12, bf16[1088,256]{1,0:T(8,128)(2,1)} %bitcast.13), custom_call_target="tpu_custom_call" | custom-call | flops 3992977408 | bytes 8388608 | tf_op jit(solution)/shard_map/pallas_call | solution.py:374
  113.8 1.9 %copy.10 = bf16[1,256,1088]{1,2,0:T(8,128)(2,1)} copy(bf16[1,256,1088]{1,2,0:T(8,128)(2,1)} %bitcast.11) | data formatting | bytes 1114112
  115.7 1.1 copy.11
